TPU v7x, 32 devices: a whole 2x2x4 slice. The times are simulated.
32 devices in a mesh: parts: 2 (over y), shard: 2 (over core), blk: 8 (over z, x).
Axes of the slice: x: 2, y: 2, z: 4, core: 2. Of those that a mesh axis runs over, the one named last changes fastest.
Arguments:
- queries_in: bfloat16 [4096, 1024], P(('parts', 'shard', 'blk')), parts along dimension 0, may hold values from -12 to 12
- query_weight: bfloat16 [1024, 1024], replicated, may hold values from -0.1875 to 0.1875
- bank: bfloat16 [2048, 1024], P(('parts', 'shard', 'blk')), parts along dimension 0, may hold values from -110 to 110
- uses: int32 [4096, 2], P(('parts', 'shard', 'blk')), parts along dimension 0, may hold values from 0 to 1, as said below
Outputs:
- retrieved: bfloat16 [4096, 1024], P(('parts', 'shard', 'blk')), parts along dimension 0
There are 2 independent parts, one for each index of `parts`. A program takes and returns all parts, laid end to end along the dimension named above; an argument that names none is the same for every part. Nothing has to cross between parts.
Inputs may be any that keep to these rules, and one draw needn't show every extreme that they name: `uses`: every query lists one or both of the two shards. Of the 128 queries of one device, at most 128 list one shard, and in every draw for every index of blk the queries of both devices at that index all list one same shard.
All inputs are finite; a program needn't handle non-finite values.
Results may differ from a plain program's by a relative error of at most 0.035.
Values may be sent and summed in bfloat16 or wider, within the bound.
A program may use at most 128 MiB of HBM per device.

v0:
```python
import math
import jax
import jax.numpy as jnp
from jax import lax
from jax.sharding import PartitionSpec as P

HEADS = 8
HEAD_DIM = 128
NEGATIVE = -1e30


def local_xla(queries_in, query_weight, bank, uses):
    rows = queries_in.shape[0]
    projected = jnp.dot(queries_in, query_weight, preferred_element_type=jnp.float32).astype(
        jnp.bfloat16
    )
    heads = projected.reshape(rows, HEADS, HEAD_DIM)
    whole = lax.all_gather(bank, ("shard", "blk"), axis=0, tiled=True)
    shard_rows = whole.shape[0] // 2
    chunk_rows = math.gcd(shard_rows, 512)
    chunks = shard_rows // chunk_rows
    blocked = whole.reshape(2, chunks, chunk_rows, HEADS, HEAD_DIM)
    allowed = uses > 0

    def step(carry, keys):
        top_old, total_old, accum_old = carry
        scores = jnp.einsum("thd,srhd->htsr", heads, keys, preferred_element_type=jnp.float32)
        scores = jnp.where(allowed[None, :, :, None], scores * HEAD_DIM ** (-0.5), NEGATIVE)
        top = jnp.maximum(top_old, jnp.max(scores, axis=(2, 3)))
        weights = jnp.exp(scores - top[:, :, None, None])
        factor = jnp.exp(top_old - top)
        total = total_old * factor + jnp.sum(weights, axis=(2, 3))
        accum = accum_old * factor[..., None] + jnp.einsum(
            "htsr,srhd->htd", weights.astype(jnp.bfloat16), keys, preferred_element_type=jnp.float32
        )
        return ((top, total, accum), None)

    start = (
        jnp.full((HEADS, rows), NEGATIVE, jnp.float32),
        jnp.zeros((HEADS, rows), jnp.float32),
        jnp.zeros((HEADS, rows, HEAD_DIM), jnp.float32),
    )
    (top, total, accum), _ = lax.scan(step, start, blocked.transpose(1, 0, 2, 3, 4))
    out = (accum / total[..., None]).astype(jnp.bfloat16)
    return out.transpose(1, 0, 2).reshape(rows, HEADS * HEAD_DIM)


def solution(mesh):
    spec = P(("parts", "shard", "blk"), None)
    return jax.shard_map(
        local_xla, mesh=mesh, in_specs=(spec, P(), spec, spec), out_specs=spec, check_vma=False
    )
```

profile of v0, /device:TPU:0, one launch (start us, length us, event | category | flops | bytes accessed | tf_op | source)
XLA Modules:
  0.0 74.4 jit_solution(16575719060348413938)
XLA Ops:
  6.5 0.0 copy-start
  6.5 0.0 all-gather.2.cloned.1.call-start
  6.5 0.7 all-gather.2.cloned.1.call-update
  7.3 0.9 %copy-done = bf16[1024,1024]{1,0:T(8,128)(2,1)S(1)} copy-done((bf16[1024,1024]{1,0:T(8,128)(2,1)S(1)}, bf16[1024,1024]{1,0:T(8,128)(2,1)}, u32[]{:S(2)}) %copy-start) | copy-done | bytes 2097176
  8.1 1.4 %fusion.15 = bf16[16,8,8,128]{3,1,2,0:T(8,128)(2,1)S(1)} fusion(bf16[128,1024]{1,0:T(8,128)(2,1)} %param.4, bf16[1024,1024]{1,0:T(8,128)(2,1)S(1)} %copy-done), kind=kOutput, calls=%fused_computation.13 | convolution fusion | flops 268566528 | bytes 2621440 | tf_op jit(solution)/shard_map/dot_general | solution.py:14
  9.6 0.7 broadcast_compare_fusion
  10.3 43.4 %all-gather.2.cloned.1.call-done = bf16[1024,1024]{1,0:T(8,128)(2,1)} async-done(((bf16[64,1024]{1,0:T(8,128)(2,1)}), bf16[1024,1024]{1,0:T(8,128)(2,1)}) %all-gather.2.cloned.1.call-update) | async-done | bytes 2097168 | tf_op jit(solution)/shard_map/all_gather | solution.py:18
  53.7 3.6 %copy.17 = bf16[128,8,8,128]{3,2,1,0:T(8,128)(2,1)} copy(bf16[128,8,8,128]{3,1,2,0:T(8,128)(2,1)} %bitcast.31) | data formatting | bytes 4194304
  57.3 4.4 %copy.10 = bf16[2,512,8,128]{1,3,0,2:T(8,128)(2,1)} copy(bf16[2,512,8,128]{3,2,1,0:T(8,128)(2,1)} %bitcast.30) | data formatting | bytes 4194304 | tf_op jit(solution)/shard_map/while/body/jit(dynamic_index_in_dim)/squeeze | solution.py:43
  61.6 0.0 copy-start.1
  61.6 2.6 %fusion = (f32[8,128]{1,0:T(8,128)S(1)}, f32[8,128,2,512]{3,1,2,0:T(8,128)S(1)}) fusion(pred[128,2]{0,1:T(4,128)(4,1)S(1)} %broadcast_compare_fusion, bf16[2,512,8,128]{1,3,0,2:T(8,128)(2,1)} %copy.10, bf16[128,8,128,1]{2,1,0,3:T(8,128)(2,1)S(1)} %bitcast.32), kind=kOutput, calls=%fused_computation.2 | convolution fusion | flops 271580160 | bytes 6557952 | tf_op jit(solution)/shard_map/while/body/eval_jaxpr/thd,srhd->htsr/dot_general | solution.py:27
  64.3 1.1 %fusion.1 = f32[8,128]{1,0:T(8,128)S(1)} fusion(f32[8,128,2,512]{3,1,2,0:T(8,128)S(1)} %get-tuple-element.20, f32[8,128]{1,0:T(8,128)S(1)} %get-tuple-element.18, pred[128,2]{0,1:T(4,128)(4,1)S(1)} %broadcast_compare_fusion), kind=kLoop, calls=%fused_computation.3 | loop fusion | flops 4193280 | bytes 4202752 | tf_op jit(solution)/shard_map/while/body/eval_jaxpr/reduce_sum | solution.py:32
  65.4 0.0 copy-done.1
  65.4 1.3 %fusion.19 = bf16[128,8,128]{0,2,1:T(8,128)(2,1)S(1)} fusion(bf16[2,512,8,128]{1,3,0,2:T(8,128)(2,1)S(1)} %copy-done.1, f32[8,128,2,512]{3,1,2,0:T(8,128)S(1)} %get-tuple-element.20, f32[8,128]{1,0:T(8,128)S(1)} %get-tuple-element.18, pred[128,2]{0,1:T(4,128)(4,1)S(1)} %broadcast_compare_fusion, f32[128,8]{0,1:T(8,128)S(1)} %bitcast_add_fusion, ...), kind=kOutput, calls=%fused_computation.15 | convolution fusion | flops 273022976 | bytes 6566144 | tf_op jit(solution)/shard_map/while/body/eval_jaxpr/htsr,srhd->htd/dot_general | solution.py:33
  66.7 0.9 %copy.11 = bf16[128,1024]{1,0:T(8,128)(2,1)} copy(bf16[128,1024]{0,1:T(8,128)(2,1)S(1)} %bitcast.33) | data formatting | bytes 524288 | tf_op jit(solution)/shard_map/reshape | solution.py:45
  (3 shorter events, 0.1 us)
Async XLA Ops:
  6.5 1.6 %copy-start = (bf16[1024,1024]{1,0:T(8,128)(2,1)S(1)}, bf16[1024,1024]{1,0:T(8,128)(2,1)}, u32[]{:S(2)}) copy-start(bf16[1024,1024]{1,0:T(8,128)(2,1)} %param.5) | copy-start | bytes 6291460
  6.5 47.2 %all-gather.2.cloned.1.call-start = ((), (), s32[]{:S(2)}) async-start(), calls=%async_computation | async-start | bytes 2228224 | tf_op jit(solution)/shard_map/all_gather | solution.py:18
  61.6 3.8 %copy-start.1 = (bf16[2,512,8,128]{1,3,0,2:T(8,128)(2,1)S(1)}, bf16[2,512,8,128]{1,3,0,2:T(8,128)(2,1)}, u32[]{:S(2)}) copy-start(bf16[2,512,8,128]{1,3,0,2:T(8,128)(2,1)} %copy.10) | copy-start | bytes 6291460
Sparse Core Ops, SparseCore 0:
  9.6 44.0 all-gather.1
where the time goes:
time: 74.7 us; the launch traced here: 74.4 us
  waiting for transfers between devices  44.1 us (59%)
  between operations  13.4 us (18%)
  local copies, waits for them, and re-layouts  9.69 us (13%)
  matrix products  5.36 us (7%)
  other arithmetic  1.8 us (2%)
    all_gather x1, waiting for transfers between devices, local_xla(): whole = lax.all_gather(bank, ('shard', 'blk'), axis=0, tiled=True)  43.4 us
    unnamed x6, local copies, waits for them, and re-layouts  4.48 us
    squeeze x1, local copies, waits for them, and re-layouts, local_xla(): lax.scan(step, start, blocked.transpose(1, 0, 2, 3, 4))  4.36 us
    dot_general x1, matrix products, step(): jnp.einsum('thd,srhd->htsr', heads, keys, preferred_element_type=jnp.floa...  2.63 us
  transfers between devices with their start and end apart: 1, of which 1 were waited for; matrix products, arithmetic and copies ran while one was open for 3% of the time, Pallas kernels for 0%

commit v1 on v0

--- a/solution.py
+++ b/solution.py
@@ -9,13 +9,34 @@
 NEGATIVE = -1e30
 
 
+def slot_perform(u, array_dim):
+    u = jnp.moveaxis(u, 0, array_dim)
+    small = u.shape
+    after = u.reshape(
+        *small[:array_dim], small[array_dim] * small[array_dim + 1], *small[array_dim + 2 :]
+    )
+    return after
+
+
+def convert_the_racks(target, along_axis):
+    world = jax.lax.axis_size(along_axis)
+    w2 = target[None]
+    for p in range(world.bit_length() - 1):
+        t1 = 1 << p
+        r1 = jax.lax.ppermute(w2, along_axis, [(hop_no, hop_no ^ t1) for hop_no in range(world)])
+        vec_out = jnp.stack([w2, r1], axis=0)
+        side_arr = jax.lax.axis_index(along_axis) >> p & 1
+        w2 = jnp.where(side_arr == 0, vec_out, vec_out[::-1]).reshape(-1, *target.shape)
+    return w2
+
+
 def local_xla(queries_in, query_weight, bank, uses):
     rows = queries_in.shape[0]
     projected = jnp.dot(queries_in, query_weight, preferred_element_type=jnp.float32).astype(
         jnp.bfloat16
     )
     heads = projected.reshape(rows, HEADS, HEAD_DIM)
-    whole = lax.all_gather(bank, ("shard", "blk"), axis=0, tiled=True)
+    whole = slot_perform(convert_the_racks(bank, ("shard", "blk")), 0)
     shard_rows = whole.shape[0] // 2
     chunk_rows = math.gcd(shard_rows, 512)
     chunks = shard_rows // chunk_rows

time: 74.7 us -> 57.6 us (0.77)
  between operations: 13.4 us -> 0.15 us
  waiting for transfers between devices: 44.1 us -> 33.4 us
  starting transfers between devices: 0.01 us -> 7.49 us
  other arithmetic: 1.8 us -> 4.66 us
  local copies, waits for them, and re-layouts: 9.69 us -> 7.21 us
  matrix products: 5.36 us -> 4.43 us
    all_gather x1 -> x0, waiting for transfers between devices: 43.4 us -> none  [local_xla(): whole = lax.all_gather(bank, ('shard', 'blk'), axis=0, tiled=True)]
    ppermute x0 -> x4, waiting for transfers between devices: none -> 33.4 us  [convert_the_racks(): jax.lax.ppermute(w2, along_axis, [(hop_no, hop_no ^ t1) for hop_no in ran...]
    ppermute x0 -> x4, starting transfers between devices: none -> 7.49 us  [convert_the_racks(): jax.lax.ppermute(w2, along_axis, [(hop_no, hop_no ^ t1) for hop_no in ran...]
    another operation x0 -> x5, other arithmetic: none -> 2.56 us  [convert_the_racks(): vec_out = jnp.stack([w2, r1], axis=0)]
    unnamed x6 -> x10, local copies, waits for them, and re-layouts: 4.48 us -> 2.03 us
    select_n x0 -> x3, other arithmetic: none -> 0.98 us  [convert_the_racks(): jnp.where(side_arr == 0, vec_out, vec_out[::-1]).reshape(-1, *target.shape)]
    dot_general x1, matrix products: 1.39 us -> 0.45 us  [local_xla(): jnp.dot(queries_in, query_weight, preferred_element_type=jnp.float32)]
  transfers between devices with their start and end apart: 1 -> 4, of which waited for: 1 -> 4; matrix products, arithmetic and copies ran while one was open for 3% -> 1% of each run, Pallas kernels for 0% -> 0%
where the time goes in v1:
time: 57.6 us; the launch traced here: 57.3 us
  waiting for transfers between devices  33.4 us (58%)
  starting transfers between devices  7.49 us (13%)
  local copies, waits for them, and re-layouts  7.21 us (13%)
  other arithmetic  4.66 us (8%)
  matrix products  4.43 us (8%)
    ppermute x4, waiting for transfers between devices, convert_the_racks(): jax.lax.ppermute(w2, along_axis, [(hop_no, hop_no ^ t1) for hop_no in ran...  33.4 us
    ppermute x4, starting transfers between devices, convert_the_racks(): jax.lax.ppermute(w2, along_axis, [(hop_no, hop_no ^ t1) for hop_no in ran...  7.49 us
    squeeze x1, local copies, waits for them, and re-layouts, local_xla(): lax.scan(step, start, blocked.transpose(1, 0, 2, 3, 4))  4.33 us
    dot_general x1, matrix products, step(): jnp.einsum('thd,srhd->htsr', heads, keys, preferred_element_type=jnp.floa...  2.66 us
    another operation x5, other arithmetic, convert_the_racks(): vec_out = jnp.stack([w2, r1], axis=0)  2.56 us
    unnamed x10, local copies, waits for them, and re-layouts  2.03 us
    dot_general x1, matrix products, step(): jnp.einsum('htsr,srhd->htd', weights.astype(jnp.bfloat16), keys, preferre...  1.33 us
  transfers between devices with their start and end apart: 4, of which 4 were waited for; matrix products, arithmetic and copies ran while one was open for 1% of the time, Pallas kernels for 0%

profile of v1, /device:TPU:0, one launch (start us, length us, event | category | flops | bytes accessed | tf_op | source)
XLA Modules:
  0.0 57.3 jit_solution(2247079728328759645)
XLA Ops:
  0.0 0.0 copy-start
  0.0 0.0 copy-start.2
  0.0 2.9 %collective-permute-start = (bf16[1,64,1024]{2,1,0:T(8,128)(2,1)}, bf16[1,64,1024]{2,1,0:T(8,128)(2,1)S(1)}, u32[]{:S(2)}, u32[]{:S(2)}) collective-permute-start(bf16[1,64,1024]{2,1,0:T(8,128)(2,1)} %bitcast.56), channel_id=1, source_target_pairs={{0,1},{1,0},{2,3},{3,2},{4,5},{5,4},{6,7},{7,6},{8,9},{9,8},{10,11... | collective-permute-start | bytes 393224 | tf_op jit(solution)/shard_map/ppermute | solution.py:26
  2.9 3.7 %collective-permute-done = bf16[1,64,1024]{2,1,0:T(8,128)(2,1)S(1)} collective-permute-done((bf16[1,64,1024]{2,1,0:T(8,128)(2,1)}, bf16[1,64,1024]{2,1,0:T(8,128)(2,1)S(1)}, u32[]{:S(2)}, u32[]{:S(2)}) %collective-permute-start) | collective-permute-done | bytes 131104 | tf_op jit(solution)/shard_map/ppermute | solution.py:26
  6.6 0.9 %pad_maximum_fusion.3 = bf16[2,1,64,1024]{3,2,1,0:T(8,128)(2,1)S(1)} fusion(bf16[1,1,64,1024]{3,2,1,0:T(8,128)(2,1)S(1)} %bitcast.58, bf16[1,1,64,1024]{3,2,1,0:T(8,128)(2,1)} %bitcast.57), kind=kLoop, calls=%fused_computation.23 | loop fusion | flops 131072 | bytes 524288 | tf_op jit(solution)/shard_map/stack | solution.py:27
  7.6 0.1 fusion.25
  7.7 1.9 %collective-permute-start.1 = (bf16[2,64,1024]{2,1,0:T(8,128)(2,1)S(1)}, bf16[2,64,1024]{2,1,0:T(8,128)(2,1)S(1)}, u32[]{:S(2)}, u32[]{:S(2)}) collective-permute-start(bf16[2,64,1024]{2,1,0:T(8,128)(2,1)S(1)} %get-tuple-element.18), channel_id=1, source_target_pairs={{0,2},{1,3},{2,0},{3,1},{4,6},{5,7},{6,4},{7,5},{8,10},{9,11},{10,... | collective-permute-start | bytes 786440 | tf_op jit(solution)/shard_map/ppermute | solution.py:26
  9.6 5.7 %collective-permute-done.1 = bf16[2,64,1024]{2,1,0:T(8,128)(2,1)S(1)} collective-permute-done((bf16[2,64,1024]{2,1,0:T(8,128)(2,1)S(1)}, bf16[2,64,1024]{2,1,0:T(8,128)(2,1)S(1)}, u32[]{:S(2)}, u32[]{:S(2)}) %collective-permute-start.1) | collective-permute-done | bytes 262176 | tf_op jit(solution)/shard_map/ppermute | solution.py:26
  15.2 0.1 pad_maximum_fusion.2
  15.3 0.0 copy-start.3
  15.3 0.1 reverse_select_fusion.2
  15.4 2.6 %collective-permute-start.2 = (bf16[4,64,1024]{2,1,0:T(8,128)(2,1)S(1)}, bf16[4,64,1024]{2,1,0:T(8,128)(2,1)S(1)}, u32[]{:S(2)}, u32[]{:S(2)}) collective-permute-start(bf16[4,64,1024]{2,1,0:T(8,128)(2,1)S(1)} %bitcast.50), channel_id=1, source_target_pairs={{0,4},{1,5},{2,6},{3,7},{4,0},{5,1},{6,2},{7,3},{8,12},{9,13},{10,... | collective-permute-start | bytes 1572872 | tf_op jit(solution)/shard_map/ppermute | solution.py:26
  18.0 21.8 %collective-permute-done.2 = bf16[4,64,1024]{2,1,0:T(8,128)(2,1)S(1)} collective-permute-done((bf16[4,64,1024]{2,1,0:T(8,128)(2,1)S(1)}, bf16[4,64,1024]{2,1,0:T(8,128)(2,1)S(1)}, u32[]{:S(2)}, u32[]{:S(2)}) %collective-permute-start.2) | collective-permute-done | bytes 524320 | tf_op jit(solution)/shard_map/ppermute | solution.py:26
  39.8 0.1 pad_maximum_fusion.1
  39.9 0.3 reverse_select_fusion.1
  40.2 0.1 collective-permute-start.3
  40.3 0.0 copy-done
  40.3 0.0 copy-done.2
  40.3 0.4 fusion.15
  40.8 0.0 copy-done.3
  40.8 2.2 %collective-permute-done.3 = bf16[8,64,1024]{2,1,0:T(8,128)(2,1)} collective-permute-done((bf16[8,64,1024]{2,1,0:T(8,128)(2,1)S(1)}, bf16[8,64,1024]{2,1,0:T(8,128)(2,1)}, u32[]{:S(2)}, u32[]{:S(2)}) %collective-permute-start.3) | collective-permute-done | bytes 1048608 | tf_op jit(solution)/shard_map/ppermute | solution.py:26
  43.0 1.4 %pad_maximum_fusion = bf16[2,8,64,1024]{3,2,1,0:T(8,128)(2,1)S(1)} fusion(bf16[1,8,64,1024]{3,2,1,0:T(8,128)(2,1)} %bitcast.12, bf16[1,8,64,1024]{3,2,1,0:T(8,128)(2,1)S(1)} %bitcast.49), kind=kLoop, calls=%fused_computation.7 | loop fusion | flops 1048576 | bytes 4194304 | tf_op jit(solution)/shard_map/stack | solution.py:27
  44.4 0.6 %reverse_select_fusion = bf16[2,8,64,1024]{3,2,1,0:T(8,128)(2,1)S(1)} fusion(bf16[2,8,64,1024]{3,2,1,0:T(8,128)(2,1)S(1)} %pad_maximum_fusion, pred[]{:T(512)S(6)} %eq.12), kind=kLoop, calls=%fused_computation.5 | loop fusion | flops 1048576 | bytes 4194305 | tf_op jit(solution)/shard_map/jit(_where)/select_n | solution.py:29
  45.1 2.0 %copy.17 = bf16[128,8,8,128]{3,2,1,0:T(8,128)(2,1)} copy(bf16[128,8,8,128]{3,1,2,0:T(8,128)(2,1)S(1)} %bitcast.46) | data formatting | bytes 4194304
  47.0 4.3 %copy.10 = bf16[2,512,8,128]{1,3,0,2:T(8,128)(2,1)} copy(bf16[2,512,8,128]{3,2,1,0:T(8,128)(2,1)} %bitcast.47) | data formatting | bytes 4194304 | tf_op jit(solution)/shard_map/while/body/jit(dynamic_index_in_dim)/squeeze | solution.py:64
  51.4 0.0 copy-start.1
  51.4 2.7 %fusion = (f32[8,128]{1,0:T(8,128)S(1)}, f32[8,128,2,512]{3,1,2,0:T(8,128)S(1)}) fusion(pred[128,2]{0,1:T(4,128)(4,1)S(1)} %broadcast_compare_fusion, bf16[2,512,8,128]{1,3,0,2:T(8,128)(2,1)} %copy.10, bf16[128,8,128,1]{2,1,0,3:T(8,128)(2,1)S(1)} %bitcast.52), kind=kOutput, calls=%fused_computation.2 | convolution fusion | flops 271580160 | bytes 6557952 | tf_op jit(solution)/shard_map/while/body/eval_jaxpr/thd,srhd->htsr/dot_general | solution.py:48
  54.0 1.1 %fusion.1 = f32[8,128]{1,0:T(8,128)S(1)} fusion(f32[8,128,2,512]{3,1,2,0:T(8,128)S(1)} %get-tuple-element.30, f32[8,128]{1,0:T(8,128)S(1)} %get-tuple-element.20, pred[128,2]{0,1:T(4,128)(4,1)S(1)} %broadcast_compare_fusion), kind=kLoop, calls=%fused_computation.3 | loop fusion | flops 4193280 | bytes 4202752 | tf_op jit(solution)/shard_map/while/body/eval_jaxpr/reduce_sum | solution.py:53
  55.1 0.0 copy-done.1
  55.1 1.3 %fusion.19 = bf16[128,8,128]{0,2,1:T(8,128)(2,1)S(1)} fusion(bf16[2,512,8,128]{1,3,0,2:T(8,128)(2,1)S(1)} %copy-done.1, f32[8,128,2,512]{3,1,2,0:T(8,128)S(1)} %get-tuple-element.30, f32[8,128]{1,0:T(8,128)S(1)} %get-tuple-element.20, pred[128,2]{0,1:T(4,128)(4,1)S(1)} %broadcast_compare_fusion, f32[128,8]{0,1:T(8,128)S(1)} %bitcast_add_fusion, ...), kind=kOutput, calls=%fused_computation.19 | convolution fusion | flops 273022976 | bytes 6566144 | tf_op jit(solution)/shard_map/while/body/eval_jaxpr/htsr,srhd->htd/dot_general | solution.py:54
  56.5 0.9 %copy.11 = bf16[128,1024]{1,0:T(8,128)(2,1)} copy(bf16[128,1024]{0,1:T(8,128)(2,1)S(1)} %bitcast.54) | data formatting | bytes 524288 | tf_op jit(solution)/shard_map/reshape | solution.py:66
  (4 shorter events, 0.1 us)
Async XLA Ops:
  0.0 40.3 %copy-start = (bf16[1024,1024]{1,0:T(8,128)(2,1)S(1)}, bf16[1024,1024]{1,0:T(8,128)(2,1)}, u32[]{:S(2)}) copy-start(bf16[1024,1024]{1,0:T(8,128)(2,1)} %param.5) | copy-start | bytes 6291460
  0.0 40.3 %copy-start.2 = (bf16[128,1024]{1,0:T(8,128)(2,1)S(1)}, bf16[128,1024]{1,0:T(8,128)(2,1)}, u32[]{:S(2)}) copy-start(bf16[128,1024]{1,0:T(8,128)(2,1)} %param.4) | copy-start | bytes 786436
  0.0 6.6 %collective-permute-start = (bf16[1,64,1024]{2,1,0:T(8,128)(2,1)}, bf16[1,64,1024]{2,1,0:T(8,128)(2,1)S(1)}, u32[]{:S(2)}, u32[]{:S(2)}) collective-permute-start(bf16[1,64,1024]{2,1,0:T(8,128)(2,1)} %bitcast.56), channel_id=1, source_target_pairs={{0,1},{1,0},{2,3},{3,2},{4,5},{5,4},{6,7},{7,6},{8,9},{9,8},{10,11... | collective-permute-start | bytes 393224 | tf_op jit(solution)/shard_map/ppermute | solution.py:26
  7.7 7.6 %collective-permute-start.1 = (bf16[2,64,1024]{2,1,0:T(8,128)(2,1)S(1)}, bf16[2,64,1024]{2,1,0:T(8,128)(2,1)S(1)}, u32[]{:S(2)}, u32[]{:S(2)}) collective-permute-start(bf16[2,64,1024]{2,1,0:T(8,128)(2,1)S(1)} %get-tuple-element.18), channel_id=1, source_target_pairs={{0,2},{1,3},{2,0},{3,1},{4,6},{5,7},{6,4},{7,5},{8,10},{9,11},{10,... | collective-permute-start | bytes 786440 | tf_op jit(solution)/shard_map/ppermute | solution.py:26
  15.3 25.5 %copy-start.3 = (s32[128,2]{0,1:T(2,128)S(1)}, s32[128,2]{0,1:T(2,128)}, u32[]{:S(2)}) copy-start(s32[128,2]{0,1:T(2,128)} %param.7) | copy-start | bytes 3076
  15.4 24.4 %collective-permute-start.2 = (bf16[4,64,1024]{2,1,0:T(8,128)(2,1)S(1)}, bf16[4,64,1024]{2,1,0:T(8,128)(2,1)S(1)}, u32[]{:S(2)}, u32[]{:S(2)}) collective-permute-start(bf16[4,64,1024]{2,1,0:T(8,128)(2,1)S(1)} %bitcast.50), channel_id=1, source_target_pairs={{0,4},{1,5},{2,6},{3,7},{4,0},{5,1},{6,2},{7,3},{8,12},{9,13},{10,... | collective-permute-start | bytes 1572872 | tf_op jit(solution)/shard_map/ppermute | solution.py:26
  40.2 2.9 %collective-permute-start.3 = (bf16[8,64,1024]{2,1,0:T(8,128)(2,1)S(1)}, bf16[8,64,1024]{2,1,0:T(8,128)(2,1)}, u32[]{:S(2)}, u32[]{:S(2)}) collective-permute-start(bf16[8,64,1024]{2,1,0:T(8,128)(2,1)S(1)} %bitcast.48), channel_id=1, source_target_pairs={{0,8},{1,9},{2,10},{3,11},{4,12},{5,13},{6,14},{7,15},{8,0},{9,1},... | collective-permute-start | bytes 3145736 | tf_op jit(solution)/shard_map/ppermute | solution.py:26
  51.4 3.8 %copy-start.1 = (bf16[2,512,8,128]{1,3,0,2:T(8,128)(2,1)S(1)}, bf16[2,512,8,128]{1,3,0,2:T(8,128)(2,1)}, u32[]{:S(2)}) copy-start(bf16[2,512,8,128]{1,3,0,2:T(8,128)(2,1)} %copy.10) | copy-start | bytes 6291460
